TPU v7x, 512 devices: a whole 4x4x16 slice. The times are simulated.
512 devices in a mesh: pool: 4 (over z_hi, core), dp: 16 (over y, x), head: 8 (over z_lo).
Axes of the slice: x: 4, y: 4, z: 16 (z_hi: 2, z_lo: 8; z = z_hi * 8 + z_lo), core: 2. Of those that a mesh axis runs over, the one named last changes fastest.
Arguments:
- queries: bfloat16 [256, 8192], P(('pool', 'dp'), 'head'), may hold values from -240 to 240
- fresh_kv: bfloat16 [2, 256, 1024], P(None, ('pool', 'dp'), 'head'), may hold values from -6 to 6
- key_value_pages: bfloat16 [2, 1536, 64, 1024], P(None, ('pool', 'dp'), None, 'head'), may hold values from -6 to 6
- page_table: int32 [256, 8], P(('pool', 'dp')), may hold values from 0 to 23, as said below
- lengths: int32 [256], P(('pool', 'dp')), may hold values from 1 to 512, as said below
- cache_scales: float32 [2, 8], P(None, 'head'), may hold values from 0.5 to 2
- residual: bfloat16 [256, 8192], P(('pool', 'head'), 'dp'), may hold values from -13 to 13
- out_weight: bfloat16 [8192, 8192], P('head', 'dp'), may hold values from -0.0625 to 0.0625
- norm_gain: float32 [8192], P('dp'), may hold values from 0.25 to 1.75
- gate_up: bfloat16 [2, 8192, 24576], P(None, 'dp', ('pool', 'head')), may hold values from -0.0625 to 0.0625
- down_weight: bfloat16 [24576, 8192], P(('pool', 'head'), 'dp'), may hold values from -0.0390625 to 0.0390625
Outputs:
- layer_out: bfloat16 [256, 8192], P(('pool', 'head'), 'dp')
Inputs may be any that keep to these rules, and one draw needn't show every extreme that they name: `lengths`: in each aligned block of 4 requests (one block of pages), exactly one length equals 512; every other length is at most 256. `page_table`: entries number the 24 pages of the request's own block. Over the requests of one block, the first ceil(length / 64) entries of each request are all distinct; later entries are any pages and are not read.
All inputs are finite; a program needn't handle non-finite values.
Results may differ from a plain program's by a relative error of at most 0.024.
Values may be sent and summed in bfloat16 or wider, within the bound.
A program may use at most 64 MiB of HBM per device.

v0:
```python
import math

import jax
import jax.numpy as jnp
from jax import lax
from jax.sharding import PartitionSpec as P

D = 8192
HEAD_DIM = 128


def attend_local(queries, fresh_kv, pages, table, lengths, scales):
    rows = queries.shape[0]
    heads = scales.shape[1]
    group = queries.shape[1] // (heads * HEAD_DIM)
    span = table.shape[1] * pages.shape[2]
    keys = pages[0][table].reshape(rows, span, heads, HEAD_DIM)
    values = pages[1][table].reshape(rows, span, heads, HEAD_DIM)
    asked = queries.reshape(rows, heads, group, HEAD_DIM)
    fresh_keys = fresh_kv[0].reshape(rows, heads, HEAD_DIM)
    fresh_values = fresh_kv[1].reshape(rows, heads, HEAD_DIM)
    factor = 1.0 / math.sqrt(HEAD_DIM)
    scores = (
        jnp.einsum("bhgd,bshd->bhgs", asked, keys, preferred_element_type=jnp.float32)
        * (scales[0] * factor)[None, :, None, None]
    )
    own = (
        jnp.einsum("bhgd,bhd->bhg", asked, fresh_keys, preferred_element_type=jnp.float32) * factor
    )
    live = jnp.arange(span, dtype=jnp.int32)[None, None, None, :] < lengths[:, None, None, None]
    top = jnp.maximum(jnp.max(jnp.where(live, scores, -jnp.inf), axis=3), own)
    weights = jnp.where(live, jnp.exp(scores - top[..., None]), 0.0)
    own_weight = jnp.exp(own - top)
    total = jnp.sum(weights, axis=3) + own_weight
    probs = (weights / total[..., None]).astype(jnp.bfloat16)
    own_prob = (own_weight / total).astype(jnp.bfloat16)
    mixed = (
        jnp.einsum("bhgs,bshd->bhgd", probs, values, preferred_element_type=jnp.float32)
        * scales[1][None, :, None, None]
    )
    mixed = (
        mixed
        + own_prob.astype(jnp.float32)[..., None] * fresh_values.astype(jnp.float32)[:, :, None, :]
    )
    return mixed.reshape(rows, heads * group * HEAD_DIM).astype(jnp.bfloat16)


def body(
    queries,
    fresh_kv,
    key_value_pages,
    page_table,
    lengths,
    cache_scales,
    residual,
    out_weight,
    norm_gain,
    gate_up,
    down_weight,
):
    attended = attend_local(queries, fresh_kv, key_value_pages, page_table, lengths, cache_scales)
    projected = jnp.dot(
        lax.all_gather(attended, "dp", axis=0, tiled=True),
        out_weight,
        preferred_element_type=jnp.float32,
    )
    summed = lax.psum_scatter(
        projected.astype(jnp.bfloat16), "head", scatter_dimension=0, tiled=True
    ).astype(jnp.float32)
    stream = residual.astype(jnp.float32) + summed
    squares = lax.psum(jnp.sum(stream * stream, axis=1), "dp")
    normed = (stream * lax.rsqrt(squares / D + 1e-06)[:, None] * norm_gain[None, :]).astype(
        jnp.bfloat16
    )
    partials = jnp.einsum(
        "tk,gkf->gtf",
        lax.all_gather(normed, ("pool", "head"), axis=0, tiled=True),
        gate_up,
        preferred_element_type=jnp.float32,
    )
    shares = lax.psum_scatter(
        partials.astype(jnp.bfloat16), "dp", scatter_dimension=1, tiled=True
    ).astype(jnp.float32)
    own_hidden = (jax.nn.silu(shares[0]) * shares[1]).astype(jnp.bfloat16)
    hidden = lax.all_gather(own_hidden, "dp", axis=0, tiled=True)
    lowered = lax.psum_scatter(
        jnp.dot(hidden, down_weight, preferred_element_type=jnp.float32).astype(jnp.bfloat16),
        ("pool", "head"),
        scatter_dimension=0,
        tiled=True,
    ).astype(jnp.float32)
    return (stream + lowered).astype(jnp.bfloat16)


def solution(mesh):
    placed = (
        P(("pool", "dp"), "head"),
        P(None, ("pool", "dp"), "head"),
        P(None, ("pool", "dp"), None, "head"),
        P(("pool", "dp"), None),
        P(("pool", "dp")),
        P(None, "head"),
        P(("pool", "head"), "dp"),
        P("head", "dp"),
        P("dp"),
        P(None, "dp", ("pool", "head")),
        P(("pool", "head"), "dp"),
    )
    return jax.shard_map(
        body, mesh=mesh, in_specs=placed, out_specs=P(("pool", "head"), "dp"), check_vma=False
    )
```

profile of v0, /device:TPU:1, one launch (start us, length us, event | category | flops | bytes accessed | tf_op | source)
XLA Modules:
  0.0 547.8 jit_solution(13271201404521397575)
XLA Ops:
  6.6 1.3 slice_bitcast_fusion.1
  8.1 0.6 fusion.21
  8.7 0.6 bitcast_convert_fusion
  9.3 0.6 gather_fusion
  10.6 0.1 fusion.12
  10.7 0.3 select_reduce_fusion
  11.1 0.2 bitcast_reduce_fusion
  11.2 0.6 fusion.18
  11.9 0.6 gather_fusion.1
  12.5 1.7 fusion.2
  14.2 19.6 %all-gather = bf16[16,4,1024]{2,1,0:T(4,128)(2,1)S(1)} all-gather(bf16[1,4,1024]{2,1,0:T(4,128)(2,1)S(1)} %reshape.138), channel_id=1, replica_groups=mesh['pool'=4,'dp'=16,'head'=8] {'dp'}, dimensions={0}, use_global_device_ids=true | all-gather | bytes 139264 | tf_op jit(solution)/shard_map/all_gather | solution.py:63
  33.8 0.9 convolution_convert_fusion.2
  34.8 65.0 %reduce-scatter.4.cloned.1.call-done = bf16[8,512]{1,0:T(8,128)(2,1)} async-done(((bf16[64,512]{1,0:T(8,128)(2,1)}), bf16[8,512]{1,0:T(8,128)(2,1)}) %reduce-scatter.4.cloned.1.call-update) | async-done | bytes 8208 | tf_op jit(solution)/shard_map/reduce_scatter | solution.py:67
  99.9 0.8 multiply_reduce_fusion
  100.7 33.2 %psum.7 = f32[8]{0:T(128)S(1)} all-reduce(f32[8]{0:T(128)S(1)} %multiply_reduce_fusion), channel_id=1, replica_groups=mesh['pool'=4,'dp'=16,'head'=8] {'dp'}, use_global_device_ids=true, to_apply=%region_4.5 | all-reduce | flops 8 | bytes 64 | tf_op jit(solution)/shard_map/psum | solution.py:71
  133.8 0.8 multiply_convert_fusion
  134.6 103.3 %all_gather.10 = bf16[256,512]{1,0:T(8,128)(2,1)S(1)} all-gather(bf16[8,512]{1,0:T(8,128)(2,1)S(1)} %multiply_convert_fusion), channel_id=1, replica_groups=mesh['pool'=4,'dp'=16,'head'=8] {'pool','head'}, dimensions={0}, use_global_device_ids=true | all-gather | bytes 270336 | tf_op jit(solution)/shard_map/all_gather | solution.py:77
  237.9 1.5 fusion
  239.5 81.8 %reduce-scatter.6.cloned.1.call-done = bf16[2,16,768]{2,1,0:T(8,128)(2,1)} async-done(((bf16[2,256,768]{2,1,0:T(8,128)(2,1)}), bf16[2,16,768]{2,1,0:T(8,128)(2,1)}) %reduce-scatter.6.cloned.1.call-update) | async-done | bytes 49168 | tf_op jit(solution)/shard_map/reduce_scatter | solution.py:81
  321.3 0.8 convert_element_type.76
  322.1 17.1 %all_gather.11 = bf16[256,768]{1,0:T(8,128)(2,1)S(1)} all-gather(bf16[16,768]{1,0:T(8,128)(2,1)S(1)} %fusion.6), channel_id=1, replica_groups=mesh['pool'=4,'dp'=16,'head'=8] {'dp'}, dimensions={0}, use_global_device_ids=true | all-gather | bytes 417792 | tf_op jit(solution)/shard_map/all_gather | solution.py:85
  339.2 1.1 convolution_convert_fusion.1
  340.3 199.7 %reduce-scatter.8.cloned.1.call-done = bf16[8,512]{1,0:T(8,128)(2,1)} async-done(((bf16[256,512]{1,0:T(8,128)(2,1)}), bf16[8,512]{1,0:T(8,128)(2,1)}) %reduce-scatter.8.cloned.1.call-update) | async-done | bytes 8208 | tf_op jit(solution)/shard_map/reduce_scatter | solution.py:86
  540.0 1.3 add_convert_fusion
  (41 shorter events, 0.5 us)
Async XLA Ops:
  6.5 231.4 %copy-start = (bf16[2,512,768]{2,1,0:T(8,128)(2,1)S(1)}, bf16[2,512,768]{2,1,0:T(8,128)(2,1)}, u32[]{:S(2)}) copy-start(bf16[2,512,768]{2,1,0:T(8,128)(2,1)} %param.20) | copy-start | bytes 4718596
  6.5 1.3 copy-start.8
  6.5 1.5 copy-start.12
  6.5 1.5 copy-start.10
  6.5 2.1 copy-start.9
  6.5 4.0 copy-start.6
  6.6 93.3 %reduce-scatter.4.cloned.1.call-start = ((), (), s32[]{:S(2)}) async-start(), calls=%async_computation.3 | async-start | bytes 73728 | tf_op jit(solution)/shard_map/reduce_scatter | solution.py:67
  11.0 0.8 copy-start.3
  11.0 22.8 %copy-start.1 = (bf16[1024,512]{1,0:T(8,128)(2,1)S(1)}, bf16[1024,512]{1,0:T(8,128)(2,1)}, u32[]{:S(2)}) copy-start(bf16[1024,512]{1,0:T(8,128)(2,1)} %param.18) | copy-start | bytes 3145732
  11.1 0.8 copy-start.7
  11.9 88.0 %copy-start.4 = (bf16[8,512]{1,0:T(8,128)(2,1)S(1)}, bf16[8,512]{1,0:T(8,128)(2,1)}, u32[]{:S(2)}) copy-start(bf16[8,512]{1,0:T(8,128)(2,1)} %param.17) | copy-start | bytes 24580
  12.5 121.3 %copy-start.11 = (f32[512]{0:T(512)S(1)}, f32[512]{0:T(512)}, u32[]{:S(2)}) copy-start(f32[512]{0:T(512)} %param.19) | copy-start | bytes 6148
  34.8 286.5 %reduce-scatter.6.cloned.1.call-start = ((), (), s32[]{:S(2)}) async-start(), calls=%async_computation.4 | async-start | bytes 835584 | tf_op jit(solution)/shard_map/reduce_scatter | solution.py:81
  237.9 101.3 %copy-start.2 = (bf16[768,512]{1,0:T(8,128)(2,1)S(1)}, bf16[768,512]{1,0:T(8,128)(2,1)}, u32[]{:S(2)}) copy-start(bf16[768,512]{1,0:T(8,128)(2,1)} %param.21) | copy-start | bytes 2359300
  239.4 300.5 %copy-start.5 = (bf16[8,512]{1,0:T(8,128)(2,1)S(1)}, bf16[8,512]{1,0:T(8,128)(2,1)}, u32[]{:S(2)}) copy-start(bf16[8,512]{1,0:T(8,128)(2,1)} %reduce-scatter.4.cloned.1.call-done) | copy-start | bytes 24580
  239.4 300.5 %reduce-scatter.8.cloned.1.call-start = ((), (), s32[]{:S(2)}) async-start(), calls=%async_computation.5 | async-start | bytes 270336 | tf_op jit(solution)/shard_map/reduce_scatter | solution.py:86
Sparse Core Ops, SparseCore 0:
  34.9 64.9 reduce-scatter.3
  239.6 81.6 reduce-scatter.5
  340.4 199.4 reduce-scatter.7
where the time goes:
time: 548 us
  waiting for transfers between devices  347 us (63%)
  blocking collectives  173 us (32%)
  between operations  13.9 us (3%)
  matrix products  5.58 us (1%)
    reduce_scatter x1, waiting for transfers between devices, body(): lax.psum_scatter(jnp.dot(hidden, down_weight, preferred_element_type=jnp....  200 us
    all_gather x1, blocking collectives, body(): lax.all_gather(normed, ('pool', 'head'), axis=0, tiled=True)  103 us
    reduce_scatter x1, waiting for transfers between devices, body(): lax.psum_scatter(partials.astype(jnp.bfloat16), 'dp', scatter_dimension=1...  81.8 us
    reduce_scatter x1, waiting for transfers between devices, body(): lax.psum_scatter(projected.astype(jnp.bfloat16), 'head', scatter_dimensio...  65 us
    psum x1, blocking collectives, body(): squares = lax.psum(jnp.sum(stream * stream, axis=1), 'dp')  33.2 us
    all_gather x1, blocking collectives, body(): lax.all_gather(attended, 'dp', axis=0, tiled=True)  19.6 us
    all_gather x1, blocking collectives, body(): hidden = lax.all_gather(own_hidden, 'dp', axis=0, tiled=True)  17.1 us
  transfers between devices with their start and end apart: 3, of which 3 were waited for; matrix products, arithmetic and copies ran while one was open for 0% of the time, Pallas kernels for 0%

commit v1 on v0

v1 whole, which is shorter than its diff:
```python
import math

import jax
import jax.numpy as jnp
from jax import lax
from jax.experimental import pallas as pl
from jax.experimental.pallas import tpu as pltpu
from jax.sharding import PartitionSpec as P

D = 8192
HEAD_DIM = 128
MESH = pl.DeviceIdType.MESH
F32 = jnp.float32
BF16 = jnp.bfloat16


def place():
    pool, dp, head = (lax.axis_index(name) for name in ("pool", "dp", "head"))
    return (pool // 2) * 8 + head, pool % 2, dp // 4, dp % 4


def device(z, core, y, x):
    return ((z // 8) * 2 + core, y * 4 + x, z % 8)


def send(src, dst, send_sem, recv_sem, to):
    pltpu.make_async_remote_copy(
        src_ref=src, dst_ref=dst, send_sem=send_sem, recv_sem=recv_sem,
        device_id=to, device_id_type=MESH,
    ).start()


def wait(ref, sem):
    pltpu.make_async_copy(ref, ref, sem).wait()


def to_tile(v):
    return jnp.concatenate([v[..., :256], v[..., 256:]], axis=-2).astype(BF16)


def from_tile(v):
    v = v.astype(F32)
    return jnp.concatenate([v[..., :8, :], v[..., 8:, :]], axis=-1)


def attend(q_ref, fresh_ref, kv, table, lengths, scales, q_rows, fresh_rows):
    q = q_ref[...].astype(F32)
    for g in range(8):
        q_rows[g * 4 : g * 4 + 4, :] = q[:, g * 128 : (g + 1) * 128]
    fresh = fresh_ref[...].astype(F32)
    for i in range(2):
        fresh_rows[i, 0:4, :] = fresh[i]
        fresh_rows[i, 4:8, :] = fresh[i]
    asked = q_rows[...]
    row = lax.broadcasted_iota(jnp.int32, (8, 1), 0) & 3
    column = lax.broadcasted_iota(jnp.int32, (8, 1536), 1)
    page, line = column >> 6, column & 63

    def by_request(values):
        a, b, c, d = values
        return jnp.where(row == 0, a, jnp.where(row == 1, b, jnp.where(row == 2, c, d)))

    length = by_request([lengths[t] for t in range(4)])
    live = jnp.zeros((8, 1536), jnp.bool_)
    for j in range(8):
        entry = by_request([table[t, j] for t in range(4)])
        live = live | ((page == entry) & (line < length - 64 * j))
    factor = 1.0 / math.sqrt(HEAD_DIM)
    keys = kv[0].reshape(1536, 128)
    scores = lax.dot_general(
        asked.astype(BF16), keys, (((1,), (1,)), ((), ())), preferred_element_type=F32
    ) * (scales[0, 0] * factor)
    scores = jnp.where(live[None], scores.reshape(4, 8, 1536), -jnp.inf)
    own = jnp.sum(asked.reshape(4, 8, 128) * fresh_rows[0][None], axis=2, keepdims=True) * factor
    top = jnp.maximum(jnp.max(scores, axis=2, keepdims=True), own)
    e = jnp.exp(scores - top)
    e_own = jnp.exp(own - top)
    total = jnp.sum(e, axis=2, keepdims=True) + e_own
    probs = (e / total).astype(BF16)
    own_prob = (e_own / total).astype(BF16).astype(F32)
    mixed = jnp.dot(
        probs.reshape(32, 1536), kv[1].reshape(1536, 128), preferred_element_type=F32
    ) * scales[1, 0]
    mixed = mixed.reshape(4, 8, 128) + own_prob * fresh_rows[1][None]
    return mixed.reshape(32, 128).astype(BF16)


def kernel(
    q_ref, fresh_ref, pages_hbm, table, lengths, scales, residual_ref, out_w_hbm, gain_ref,
    gate_up_hbm, down_hbm, out_ref,
    kv, out_w, gate_up, down, q_rows, fresh_rows, att, b_send, b_recv, stream, normed,
    d_send, d_recv, sq_part, sq_send, sq_recv, hidden, g_own, sib_send, sib_recv,
    g1_send, g1_recv, g1_own, g2_send, g2_recv,
    load_sem, a_sem, b_sem, c_sem, d_sem, sq_sem, h_sem, sib_sem, g1_sem, g2_sem,
):
    z, core, y, x = place()
    dp = y * 4 + x
    head = z % 8
    cls, block = z % 4, z // 4

    loads = []
    for i, (src, dst) in enumerate(
        ((pages_hbm, kv), (out_w_hbm, out_w), (gate_up_hbm, gate_up), (down_hbm, down))
    ):
        loads.append(pltpu.make_async_copy(src, dst, load_sem.at[i]))
        loads[-1].start()

    def plane(k):
        return device(z, core, (y + k // 4) % 4, (x + k % 4) % 4)

    def line(k):
        return device((z // 8) * 8 + (head + k) % 8, core, y, x)

    def ring(k):
        return device((z + k + 16) % 16, core, y, x)

    sibling = device(z, 1 - core, y, x)

    barrier = pltpu.get_barrier_semaphore()

    def greet(to):
        pl.semaphore_signal(barrier, inc=1, device_id=to, device_id_type=MESH)

    for k in range(1, 16):
        greet(plane(k))
    for k in range(1, 8):
        greet(line(k))
    for k in (1, -1, 2, -2, 4, -4, 8):
        greet(ring(k))
    greet(sibling)

    loads[0].wait()
    att[dp] = attend(q_ref, fresh_ref, kv, table, lengths, scales, q_rows, fresh_rows)
    pl.semaphore_wait(barrier, 30)
    for k in range(1, 16):
        send(att.at[dp], att.at[dp], a_sem.at[0], a_sem.at[1], plane(k))
    loads[1].wait()
    wait(att.at[0:15], a_sem.at[1])

    rows = att[...].astype(F32).reshape(8, 2, 4, 8, 128)
    even, odd = rows[:, 0], rows[:, 1]
    upper = lax.broadcasted_iota(jnp.int32, (8, 128), 0) < 4

    def swap(v):
        return pltpu.roll(v.reshape(32 * 8, 128).reshape(32, 8, 128), 4, 1).reshape(8, 4, 8, 128)

    low = jnp.where(upper, even, swap(odd))
    high = jnp.where(upper, swap(even), odd)
    columns = []
    for g in range(8):
        columns.append((low if g % 2 == 0 else high)[:, g // 2].reshape(64, 128))
    attended = jnp.concatenate(columns, axis=1).astype(BF16)
    projected = jnp.dot(attended, out_w[...], preferred_element_type=F32)
    b_send[...] = to_tile(projected.reshape(8, 8, 512))
    for k in range(1, 8):
        send(b_send.at[(head + k) % 8], b_recv.at[head], b_sem.at[0], b_sem.at[1], line(k))
    b_recv[head] = b_send[head]
    wait(b_recv.at[0:7], b_sem.at[1])
    summed = from_tile(jnp.sum(b_recv[...].astype(F32), axis=0))
    stream[...] = residual_ref[...].astype(F32) + summed

    gain = gain_ref[...].reshape(1, 512)
    normed[core, cls, block] = to_tile(stream[...] * gain)
    mine = normed.at[core, cls, block]
    for k in (1, 2, 3):
        send(mine, mine, c_sem.at[0], c_sem.at[1], ring(4 * k))
    wait(normed.at[0, 0, 0:3], c_sem.at[1])
    whole = normed.at[core, cls]
    send(whole, whole, c_sem.at[2], c_sem.at[3], ring(1))
    send(whole, whole, c_sem.at[2], c_sem.at[4], ring(-1))
    for i, k in ((0, 2), (1, -2)):
        half = normed.at[core, cls, 2 * i : 2 * i + 2]
        send(half, half, c_sem.at[2], c_sem.at[5], ring(k))
    send(whole, whole, c_sem.at[6], c_sem.at[7], sibling)

    inverse = 1.0 / (gain * gain)

    def feed(half, c):
        tokens = from_tile(normed[half, c]).reshape(32, 512)
        squares = tokens * tokens * inverse
        sq_part[half, c] = (
            squares[:, :128] + squares[:, 128:256] + squares[:, 256:384] + squares[:, 384:]
        ).reshape(4, 8, 128)
        lhs = tokens.astype(BF16)
        gate = jnp.dot(lhs, gate_up[0], preferred_element_type=F32).reshape(4, 8, 768)
        up = jnp.dot(lhs, gate_up[1], preferred_element_type=F32).reshape(4, 8, 768)
        d_send[half, c] = jnp.concatenate([gate, up], axis=1).astype(BF16)
        for a in range(4):
            oy, ox = a, (c + a) % 4
            same = (oy == y) & (ox == x)

            @pl.when(jnp.logical_not(same))
            def _():
                send(
                    d_send.at[half, c, a], d_recv.at[half, dp], d_sem.at[0], d_sem.at[1 + half],
                    device(z, core, oy, ox),
                )

            @pl.when(same)
            def _():
                d_recv[half, dp] = d_send[half, c, a]

    other = 1 - core
    loads[2].wait()
    feed(core, cls)
    wait(whole, c_sem.at[7])
    feed(other, cls)
    for step, (k, sem) in enumerate(((1, 4), (3, 3), (2, 5))):
        c = (cls + k) % 4
        arrived = normed.at[core, c]
        wait(arrived, c_sem.at[sem])
        send(arrived, arrived, c_sem.at[6], c_sem.at[8 + step], sibling)
        feed(core, c)
    for step, k in enumerate((1, 3, 2)):
        c = (cls + k) % 4
        wait(normed.at[other, c], c_sem.at[8 + step])
        feed(other, c)

    part = sq_part[...].reshape(32, 8, 128)
    folded = part + pltpu.roll(part, 64, 2)
    left = lax.broadcasted_iota(jnp.int32, (8, 128), 1) < 64
    sq_send[...] = jnp.where(left, folded[:16], folded[16:]).reshape(4, 4, 8, 128)
    for k in range(1, 16):
        oy, ox = (y + k // 4) % 4, (x + k % 4) % 4
        send(sq_send.at[(ox - oy + 4) % 4, oy], sq_recv.at[dp], sq_sem.at[0], sq_sem.at[1], plane(k))
    own_cls = (x - y + 4) % 4
    sq_recv[dp] = sq_send[own_cls, y]

    wait(sq_recv.at[0:15], sq_sem.at[1])
    squares = jnp.sum(sq_recv[...], axis=0)
    halves = []
    for half in range(2):
        wait(d_recv.at[0, 0:15], d_sem.at[1 + half])
        total = jnp.sum(d_recv[half].astype(F32), axis=0)
        mean = jnp.sum(jnp.where(left == (half == 0), squares, 0.0), axis=1, keepdims=True) / D
        scale = lax.rsqrt(mean + 1e-6)
        gate, up = total[:8] * scale, total[8:] * scale
        halves.append(gate / (1.0 + jnp.exp(-gate)) * up)
    hidden[own_cls, y] = jnp.concatenate(halves, axis=0).astype(BF16)
    mine = hidden.at[own_cls, y]
    for k in range(1, 16):
        send(mine, mine, h_sem.at[0], h_sem.at[1], plane(k))
    loads[3].wait()
    wait(d_recv.at[0, 0:15], h_sem.at[1])

    for k in (2, 1, 3, 0):
        c = (cls + k) % 4
        lowered = jnp.dot(hidden[c].reshape(64, 768), down[...], preferred_element_type=F32)
        lowered = lowered.reshape(4, 16, 512)
        first = core == 0
        g_own[c] = jnp.where(first, lowered[:, :8], lowered[:, 8:])
        sib_send[c] = to_tile(jnp.where(first, lowered[:, 8:], lowered[:, :8]))
        send(sib_send.at[c], sib_recv.at[c], sib_sem.at[0], sib_sem.at[1 + k], sibling)
    for k in (2, 1, 3, 0):
        c = (cls + k) % 4
        wait(sib_recv.at[c], sib_sem.at[1 + k])
        both = g_own[c] + from_tile(sib_recv[c])
        if k == 0:
            g1_own[...] = both
            continue
        g1_send[k - 1] = to_tile(both)
        if k == 2:
            for i, to in ((0, 2), (1, -2)):
                part = pl.ds(2 * i, 2)
                send(g1_send.at[1, part], g1_recv.at[1, part], g1_sem.at[0], g1_sem.at[2], ring(to))
        else:
            send(g1_send.at[k - 1], g1_recv.at[k - 1], g1_sem.at[0], g1_sem.at[k], ring(2 - k))
    total = g1_own[...]
    for k in (1, 3, 2):
        wait(g1_recv.at[k - 1], g1_sem.at[k])
        total = total + from_tile(g1_recv[k - 1])
    g1_own[...] = total
    g2_send[...] = to_tile(total)
    for k in (1, 2, 3):
        send(g2_send.at[(block + k) % 4], g2_recv.at[k - 1], g2_sem.at[0], g2_sem.at[1], ring(4 * k))
    wait(g2_recv, g2_sem.at[1])
    lowered = g1_own[block] + from_tile(jnp.sum(g2_recv[...].astype(F32), axis=0))
    out_ref[...] = (stream[...] + lowered).astype(BF16)

    wait(att.at[0:15], a_sem.at[0])
    wait(b_recv.at[0:7], b_sem.at[0])
    wait(normed.at[0, 0, 0:3], c_sem.at[0])
    wait(normed.at[0, 0:3], c_sem.at[2])
    wait(normed.at[0], c_sem.at[6])
    wait(d_recv.at[:, 0:15], d_sem.at[0])
    wait(sq_recv.at[0:15], sq_sem.at[0])
    wait(d_recv.at[0, 0:15], h_sem.at[0])
    wait(sib_recv, sib_sem.at[0])
    wait(g1_recv, g1_sem.at[0])
    wait(g2_recv, g2_sem.at[0])


def body(
    queries, fresh_kv, key_value_pages, page_table, lengths, cache_scales, residual, out_weight,
    norm_gain, gate_up, down_weight,
):
    vmem = pl.BlockSpec(memory_space=pltpu.VMEM)
    smem = pl.BlockSpec(memory_space=pltpu.SMEM)
    anywhere = pl.BlockSpec(memory_space=pl.ANY)
    sems = pltpu.SemaphoreType.DMA
    return pl.pallas_call(
        kernel,
        out_shape=jax.ShapeDtypeStruct((8, 512), BF16),
        in_specs=[vmem, vmem, anywhere, smem, smem, smem, vmem, anywhere, vmem, anywhere, anywhere],
        out_specs=vmem,
        scratch_shapes=[
            pltpu.VMEM((2, 24, 64, 128), BF16),
            pltpu.VMEM((1024, 512), BF16),
            pltpu.VMEM((2, 512, 768), BF16),
            pltpu.VMEM((768, 512), BF16),
            pltpu.VMEM((32, 128), F32),
            pltpu.VMEM((2, 8, 128), F32),
            pltpu.VMEM((16, 32, 128), BF16),
            pltpu.VMEM((8, 16, 256), BF16),
            pltpu.VMEM((8, 16, 256), BF16),
            pltpu.VMEM((8, 512), F32),
            pltpu.VMEM((2, 4, 4, 16, 256), BF16),
            pltpu.VMEM((2, 4, 4, 16, 768), BF16),
            pltpu.VMEM((2, 16, 16, 768), BF16),
            pltpu.VMEM((2, 4, 4, 8, 128), F32),
            pltpu.VMEM((4, 4, 8, 128), F32),
            pltpu.VMEM((16, 8, 128), F32),
            pltpu.VMEM((4, 4, 16, 768), BF16),
            pltpu.VMEM((4, 4, 8, 512), F32),
            pltpu.VMEM((4, 4, 16, 256), BF16),
            pltpu.VMEM((4, 4, 16, 256), BF16),
            pltpu.VMEM((3, 4, 16, 256), BF16),
            pltpu.VMEM((3, 4, 16, 256), BF16),
            pltpu.VMEM((4, 8, 512), F32),
            pltpu.VMEM((4, 16, 256), BF16),
            pltpu.VMEM((3, 16, 256), BF16),
            sems((4,)), sems((2,)), sems((2,)), sems((11,)), sems((3,)), sems((2,)), sems((2,)),
            sems((5,)), sems((4,)), sems((2,)),
        ],
        compiler_params=pltpu.CompilerParams(
            collective_id=0, has_side_effects=True, vmem_limit_bytes=40 << 20
        ),
        name="decode_layer",
    )(
        queries, fresh_kv, key_value_pages, page_table, lengths, cache_scales, residual,
        out_weight, norm_gain, gate_up, down_weight,
    )


def solution(mesh):
    placed = (
        P(("pool", "dp"), "head"),
        P(None, ("pool", "dp"), "head"),
        P(None, ("pool", "dp"), None, "head"),
        P(("pool", "dp"), None),
        P(("pool", "dp")),
        P(None, "head"),
        P(("pool", "head"), "dp"),
        P("head", "dp"),
        P("dp"),
        P(None, "dp", ("pool", "head")),
        P(("pool", "head"), "dp"),
    )
    return jax.shard_map(
        body, mesh=mesh, in_specs=placed, out_specs=P(("pool", "head"), "dp"), check_vma=False
    )
```

time: 548 us -> 82.1 us (0.15)
  waiting for transfers between devices: 347 us -> 0 us
  blocking collectives: 173 us -> 0 us
  Pallas kernels: 0 us -> 71.4 us
  between operations: 13.9 us -> 0.02 us
  local copies, waits for them, and re-layouts: 3.34 us -> 10.3 us
  matrix products: 5.58 us -> 0 us
    reduce_scatter x3 -> x0, waiting for transfers between devices: 346 us -> none  [the longest x1 200 us: body(): lax.psum_scatter(jnp.dot(hidden, down_weight, preferred_element_type=jnp....]
    all_gather x3 -> x0, blocking collectives: 140 us -> none  [the longest x1 103 us: body(): lax.all_gather(normed, ('pool', 'head'), axis=0, tiled=True)]
    pallas_call x0 -> x1, Pallas kernels: none -> 71.4 us  [body(): pl.pallas_call(kernel, out_shape=jax.ShapeDtypeStruct((8, 512), BF16), in...]
    psum x1 -> x0, blocking collectives: 33.2 us -> none  [body(): squares = lax.psum(jnp.sum(stream * stream, axis=1), 'dp')]
    unnamed x28 -> x22, local copies, waits for them, and re-layouts: 0.1 us -> 10.3 us
    dot_general x6 -> x0, matrix products: 5.58 us -> none  [the longest x1 1.66 us: attend_local(): jnp.einsum('bhgs,bshd->bhgd', probs, values, preferred_element_type=jnp.f...]
  transfers between devices with their start and end apart: 3 -> 0, of which waited for: 3 -> 0; matrix products, arithmetic and copies ran while one was open for 0% -> 0% of each run, Pallas kernels for 0% -> 0%
where the time goes in v1:
time: 82.1 us; the launch traced here: 81.7 us
  Pallas kernels  71.4 us (87%)
  local copies, waits for them, and re-layouts  10.3 us (13%)
    pallas_call x1, Pallas kernels, body(): pl.pallas_call(kernel, out_shape=jax.ShapeDtypeStruct((8, 512), BF16), in...  71.4 us
    unnamed x22, local copies, waits for them, and re-layouts  10.3 us

profile of v1, /device:TPU:1, one launch (start us, length us, event | category | flops | bytes accessed | tf_op | source)
XLA Modules:
  0.0 81.7 jit_solution(15515979639448387046)
XLA Ops:
  0.0 0.7 copy.12.scales
  0.7 0.0 copy-start
  0.7 1.4 %copy-done = bf16[2,512,768]{2,1,0:T(8,128)(2,1)S(1)} copy-done((bf16[2,512,768]{2,1,0:T(8,128)(2,1)S(1)}, bf16[2,512,768]{2,1,0:T(8,128)(2,1)}, u32[]{:S(2)}) %copy-start) | copy-done | bytes 1572888
  2.1 0.0 copy-start.1
  2.2 1.2 %copy-done.1 = bf16[1024,512]{1,0:T(8,128)(2,1)S(1)} copy-done((bf16[1024,512]{1,0:T(8,128)(2,1)S(1)}, bf16[1024,512]{1,0:T(8,128)(2,1)}, u32[]{:S(2)}) %copy-start.1) | copy-done | bytes 1048600
  3.4 0.0 copy-start.2
  3.4 1.1 %copy-done.2 = bf16[2,24,64,128]{3,2,1,0:T(8,128)(2,1)S(1)} copy-done((bf16[2,24,64,128]{3,2,1,0:T(8,128)(2,1)S(1)}, bf16[2,24,64,128]{3,2,1,0:T(8,128)(2,1)}, u32[]{:S(2)}) %copy-start.2) | copy-done | bytes 786456
  4.5 0.0 copy-start.3
  4.5 1.1 %copy-done.3 = bf16[768,512]{1,0:T(8,128)(2,1)S(1)} copy-done((bf16[768,512]{1,0:T(8,128)(2,1)S(1)}, bf16[768,512]{1,0:T(8,128)(2,1)}, u32[]{:S(2)}) %copy-start.3) | copy-done | bytes 786456
  5.6 0.0 copy-start.4
  5.6 0.7 copy-done.4
  6.3 0.0 copy-start.5
  6.3 0.7 copy-done.5
  7.0 0.0 copy-start.6
  7.0 0.7 copy-done.6
  7.7 0.0 copy-start.7
  7.7 0.7 copy-done.7
  8.4 0.0 copy-start.8
  8.4 0.7 copy-done.8
  9.1 0.0 copy-start.9
  9.1 0.7 copy-done.9
  9.7 71.4 %decode_layer.1 = bf16[8,512]{1,0:T(8,128)(2,1)S(1)} custom-call(bf16[4,1024]{1,0:T(4,128)(2,1)S(1)} %copy-done.4, bf16[2,4,128]{2,1,0:T(4,128)(2,1)S(1)} %copy-done.6, bf16[2,24,64,128]{3,2,1,0:T(8,128)(2,1)S(1)} %copy-done.2, s32[4,8]{1,0:T(4,128)S(1)} %copy-done.7, s32[4]{0:T(128)S(1)} %copy-done.9, f32[2,1]{1,0:T(2,128)S(1)} %copy.12.scales, ...), custom_call_target="tpu_custom_call" | custom-call | tf_op jit(solution)/shard_map/decode_layer/pallas_call | solution.py:301
  81.1 0.6 copy.14
Async XLA Ops:
  0.7 1.4 %copy-start = (bf16[2,512,768]{2,1,0:T(8,128)(2,1)S(1)}, bf16[2,512,768]{2,1,0:T(8,128)(2,1)}, u32[]{:S(2)}) copy-start(bf16[2,512,768]{2,1,0:T(8,128)(2,1)} %gate_up_hbm.1) | copy-start | bytes 4718596
  2.1 1.2 %copy-start.1 = (bf16[1024,512]{1,0:T(8,128)(2,1)S(1)}, bf16[1024,512]{1,0:T(8,128)(2,1)}, u32[]{:S(2)}) copy-start(bf16[1024,512]{1,0:T(8,128)(2,1)} %out_w_hbm.1) | copy-start | bytes 3145732
  3.4 1.1 %copy-start.2 = (bf16[2,24,64,128]{3,2,1,0:T(8,128)(2,1)S(1)}, bf16[2,24,64,128]{3,2,1,0:T(8,128)(2,1)}, u32[]{:S(2)}) copy-start(bf16[2,24,64,128]{3,2,1,0:T(8,128)(2,1)} %pages_hbm.1) | copy-start | bytes 2359300
  4.5 1.1 %copy-start.3 = (bf16[768,512]{1,0:T(8,128)(2,1)S(1)}, bf16[768,512]{1,0:T(8,128)(2,1)}, u32[]{:S(2)}) copy-start(bf16[768,512]{1,0:T(8,128)(2,1)} %down_hbm.1) | copy-start | bytes 2359300
  5.6 0.7 copy-start.4
  6.3 0.7 copy-start.5
  7.0 0.7 copy-start.6
  7.7 0.7 copy-start.7
  8.4 0.7 copy-start.8
  9.1 0.7 copy-start.9

commit v2 on v1

v2 whole, which is shorter than its diff:
```python
import math

import jax
import jax.numpy as jnp
from jax import lax
from jax.experimental import pallas as pl
from jax.experimental.pallas import tpu as pltpu
from jax.sharding import PartitionSpec as P

D = 8192
HEAD_DIM = 128
MESH = pl.DeviceIdType.MESH
OFFSETS = (0, 1, -1, 2, -2, 3, -3, 4, -4, 5, -5, 6, -6, 7, -7, 8)
SLOT = {o % 16: i for i, o in enumerate(OFFSETS)}
GROUPS = ((0, 1), (1, 3), (3, 7), (7, 11), (11, 16))
ALONG_Z = (1, -1, 8, 7, -7, 6, -6, 5, -5, 4, -4, 3, -3, 2, -2)
NEAR = ((0, 1), (0, 3), (1, 0), (3, 0))
MIDDLE = ((0, 2), (2, 0), (1, 1), (1, 3), (3, 1), (3, 3))
FAR = ((1, 2), (2, 1), (3, 2), (2, 3), (2, 2))
F32 = jnp.float32
BF16 = jnp.bfloat16


def place():
    pool, dp, head = (lax.axis_index(name) for name in ("pool", "dp", "head"))
    return (pool // 2) * 8 + head, pool % 2, dp // 4, dp % 4


def device(z, core, y, x):
    return ((z // 8) * 2 + core, y * 4 + x, z % 8)


def send(src, dst, send_sem, recv_sem, to):
    pltpu.make_async_remote_copy(
        src_ref=src, dst_ref=dst, send_sem=send_sem, recv_sem=recv_sem,
        device_id=to, device_id_type=MESH,
    ).start()


def wait(ref, sem):
    pltpu.make_async_copy(ref, ref, sem).wait()


def to_tile(v):
    return jnp.concatenate([v[..., :256], v[..., 256:]], axis=-2).astype(BF16)


def from_tile(v):
    v = v.astype(F32)
    return jnp.concatenate([v[..., :8, :], v[..., 8:, :]], axis=-1)


def attend(q_ref, fresh_ref, kv, table, lengths, scales, q_rows, fresh_rows):
    q = q_ref[...].astype(F32)
    for g in range(8):
        q_rows[g * 4 : g * 4 + 4, :] = q[:, g * 128 : (g + 1) * 128]
    fresh = fresh_ref[...].astype(F32)
    for i in range(2):
        fresh_rows[i, 0:4, :] = fresh[i]
        fresh_rows[i, 4:8, :] = fresh[i]
    asked = q_rows[...]
    row = lax.broadcasted_iota(jnp.int32, (8, 1), 0) & 3
    column = lax.broadcasted_iota(jnp.int32, (8, 1536), 1)
    page, line = column >> 6, column & 63

    def by_request(values):
        a, b, c, d = values
        return jnp.where(row == 0, a, jnp.where(row == 1, b, jnp.where(row == 2, c, d)))

    length = by_request([lengths[t] for t in range(4)])
    live = jnp.zeros((8, 1536), jnp.bool_)
    for j in range(8):
        entry = by_request([table[t, j] for t in range(4)])
        live = live | ((page == entry) & (line < length - 64 * j))
    factor = 1.0 / math.sqrt(HEAD_DIM)
    keys = kv[0].reshape(1536, 128)
    scores = lax.dot_general(
        asked.astype(BF16), keys, (((1,), (1,)), ((), ())), preferred_element_type=F32
    ) * (scales[0, 0] * factor)
    scores = jnp.where(live[None], scores.reshape(4, 8, 1536), -jnp.inf)
    own = jnp.sum(asked.reshape(4, 8, 128) * fresh_rows[0][None], axis=2, keepdims=True) * factor
    top = jnp.maximum(jnp.max(scores, axis=2, keepdims=True), own)
    e = jnp.exp(scores - top)
    e_own = jnp.exp(own - top)
    total = jnp.sum(e, axis=2, keepdims=True) + e_own
    probs = (e / total).astype(BF16)
    own_prob = (e_own / total).astype(BF16).astype(F32)
    mixed = jnp.dot(
        probs.reshape(32, 1536), kv[1].reshape(1536, 128), preferred_element_type=F32
    ) * scales[0, 1]
    mixed = mixed.reshape(4, 8, 128) + own_prob * fresh_rows[1][None]
    return mixed.reshape(32, 128).astype(BF16)


def kernel(
    q_hbm, fresh_hbm, pages_hbm, table_hbm, lengths_hbm, scales_hbm, residual_hbm, out_w_hbm,
    gain_hbm, gate_up_hbm, down_hbm, out_ref,
    q_ref, fresh_ref, table, lengths, scales, residual_ref, gain_ref, kv, out_w, gate_up, down, q_rows, fresh_rows, att, b_send, b_recv, stream, normed,
    d_send, d_recv, sq_send, sq_recv, hidden, g_send, g_recv,
    load_sem, pair_sem, a_sem, b_sem, c_sem, d_sem, sq_sem, h_sem, g_sem,
):
    z, core, y, x = place()
    dp = y * 4 + x
    head = z % 8

    pairs = (
        (table_hbm, table), (lengths_hbm, lengths), (scales_hbm, scales), (q_hbm, q_ref),
        (fresh_hbm, fresh_ref), (pages_hbm, kv), (residual_hbm, residual_ref), (gain_hbm, gain_ref),
        (out_w_hbm, out_w), (gate_up_hbm, gate_up.at[core]), (down_hbm, down.at[core]),
    )
    loads = [
        pltpu.make_async_copy(src, dst, load_sem.at[i]) for i, (src, dst) in enumerate(pairs)
    ]
    for load in loads:
        load.start()

    def plane(dy, dx):
        return device(z, core, (y + dy) % 4, (x + dx) % 4)

    def ring(k):
        return device((z + k + 16) % 16, core, y, x)

    sibling = device(z, 1 - core, y, x)
    others = FAR[::-1] + MIDDLE + NEAR

    barrier = pltpu.get_barrier_semaphore()

    def greet(to):
        pl.semaphore_signal(barrier, inc=1, device_id=to, device_id_type=MESH)

    for k in range(1, 16):
        greet(ring(k))
    for step in others:
        greet(plane(*step))
    greet(sibling)

    for load in loads[:6]:
        load.wait()
    att[dp] = attend(q_ref, fresh_ref, kv, table, lengths, scales, q_rows, fresh_rows)
    pl.semaphore_wait(barrier, 31)
    for step in others:
        send(att.at[dp], att.at[dp], a_sem.at[0], a_sem.at[1], plane(*step))
    send(gate_up_hbm, gate_up.at[core], pair_sem.at[0], pair_sem.at[1], sibling)
    send(down_hbm, down.at[core], pair_sem.at[2], pair_sem.at[3], sibling)
    for load in loads[6:9]:
        load.wait()
    wait(att.at[0:15], a_sem.at[1])

    rows = att[...].astype(F32).reshape(8, 2, 4, 8, 128)
    even, odd = rows[:, 0], rows[:, 1]
    upper = lax.broadcasted_iota(jnp.int32, (8, 128), 0) < 4

    def swap(v):
        return pltpu.roll(v.reshape(32 * 8, 128).reshape(32, 8, 128), 4, 1).reshape(8, 4, 8, 128)

    low = jnp.where(upper, even, swap(odd))
    high = jnp.where(upper, swap(even), odd)
    columns = []
    for g in range(8):
        columns.append((low if g % 2 == 0 else high)[:, g // 2].reshape(64, 128))
    attended = jnp.concatenate(columns, axis=1).astype(BF16)
    projected = jnp.dot(attended, out_w[...], preferred_element_type=F32)
    b_send[...] = to_tile(projected.reshape(8, 8, 512))
    for i in range(7):
        up_to, down_to = 7 - i, i
        up_to = up_to - jnp.where(up_to <= head, 1, 0)
        down_to = down_to + jnp.where(down_to >= head, 1, 0)
        to = jnp.where(head < 4, up_to, down_to)
        send(b_send.at[to], b_recv.at[head], b_sem.at[0], b_sem.at[1], device((z // 8) * 8 + to, core, y, x))
    b_recv[head] = b_send[head]
    wait(b_recv.at[0:7], b_sem.at[1])
    summed = from_tile(jnp.sum(b_recv[...].astype(F32), axis=0))
    stream[...] = residual_ref[...].astype(F32) + summed

    gain = gain_ref[...].reshape(1, 512)
    normed[0] = to_tile(stream[...] * gain)
    for k in ALONG_Z:
        slot = SLOT[-k % 16]
        send(normed.at[0], normed.at[slot], c_sem.at[0], c_sem.at[slot], ring(k))

    inverse = 1.0 / (gain * gain)

    def feed(group):
        lo, hi = GROUPS[group]
        n = hi - lo
        for slot in range(max(lo, 1), hi):
            wait(normed.at[0], c_sem.at[slot])
        tokens = from_tile(normed[lo:hi]).reshape(8 * n, 512)
        squares = tokens * tokens * inverse
        squares = squares[:, :128] + squares[:, 128:256] + squares[:, 256:384] + squares[:, 384:]
        sq_send[lo:hi] = squares.reshape(n, 8, 128)
        lhs = tokens.astype(BF16)

        def both(i):
            parts = [jnp.dot(lhs, gate_up[c, i], preferred_element_type=F32) for c in range(2)]
            return jnp.concatenate(parts, axis=1).reshape(n, 8, 1536)

        d_send[lo:hi] = jnp.concatenate([both(0), both(1)], axis=1).astype(BF16)
        for slot in range(lo, hi):
            u = OFFSETS[slot] % 16
            oy, ox = u % 4, (u % 4 + u // 4) % 4
            same = dp == oy * 4 + ox

            @pl.when(jnp.logical_not(same))
            def _():
                to = device(z, core, oy, ox)
                send(d_send.at[slot], d_recv.at[dp], d_sem.at[0], d_sem.at[1], to)
                send(sq_send.at[slot], sq_recv.at[dp], sq_sem.at[0], sq_sem.at[1], to)

            @pl.when(same)
            def _():
                d_recv[dp] = d_send[slot]
                sq_recv[dp] = sq_send[slot]

    loads[9].wait()
    wait(gate_up.at[0], pair_sem.at[1])
    for group in range(5):
        feed(group)

    own = ((x - y + 4) % 4) * 4 + y
    wait(sq_recv.at[0:15], sq_sem.at[1])
    mean = jnp.sum(jnp.sum(sq_recv[...], axis=0), axis=1, keepdims=True) / D
    scale = lax.rsqrt(mean + 1e-6)
    wait(d_recv.at[0:15], d_sem.at[1])
    total = d_recv[0].astype(F32)
    for i in range(1, 16):
        total = total + d_recv[i].astype(F32)
    gate, up = total[:8] * scale, total[8:] * scale
    own_hidden = gate / (1.0 + jnp.exp(-gate)) * up
    hidden[own] = jnp.concatenate([own_hidden[:, :768], own_hidden[:, 768:]], axis=0).astype(BF16)
    mine = hidden.at[own]
    for steps, sem in ((FAR[::-1], 3), (MIDDLE, 2), (NEAR, 1)):
        for dy, dx in steps:
            send(mine, mine, h_sem.at[0], h_sem.at[sem], plane(-dy, -dx))
    loads[10].wait()
    wait(down.at[0], pair_sem.at[3])

    def lower(start, steps):
        n = len(steps)
        chips = [((x + dx - y - dy + 8) % 4) * 4 + (y + dy) % 4 for dy, dx in steps]
        tokens = jnp.concatenate([hidden[u][None] for u in chips], axis=0).astype(F32)
        lowered = jnp.zeros((8 * n, 512), F32)
        for c in range(2):
            lhs = tokens[:, 8 * c : 8 * c + 8].reshape(8 * n, 768).astype(BF16)
            lowered = lowered + jnp.dot(lhs, down[c], preferred_element_type=F32)
        g_send[pl.ds(start, n)] = to_tile(lowered.reshape(n, 8, 512))
        for i, u in enumerate(chips):

            @pl.when(u != 0)
            def _():
                send(g_send.at[start + i], g_recv.at[u], g_sem.at[0], g_sem.at[1], ring(u))

            @pl.when(u == 0)
            def _():
                g_recv[0] = g_send[start + i]

    wait(hidden.at[0:4], h_sem.at[1])
    lower(0, ((0, 0),) + NEAR)
    wait(hidden.at[0:6], h_sem.at[2])
    lower(5, MIDDLE)
    wait(hidden.at[0:5], h_sem.at[3])
    lower(11, FAR)
    wait(g_recv.at[1:16], g_sem.at[1])
    lowered = from_tile(jnp.sum(g_recv[...].astype(F32), axis=0))
    out_ref[...] = (stream[...] + lowered).astype(BF16)

    wait(gate_up.at[0], pair_sem.at[0])
    wait(down.at[0], pair_sem.at[2])
    wait(att.at[0:15], a_sem.at[0])
    wait(b_recv.at[0:7], b_sem.at[0])
    wait(normed.at[0:15], c_sem.at[0])
    wait(d_recv.at[0:15], d_sem.at[0])
    wait(sq_recv.at[0:15], sq_sem.at[0])
    wait(hidden.at[0:15], h_sem.at[0])
    wait(g_recv.at[0:15], g_sem.at[0])


def body(
    queries, fresh_kv, key_value_pages, page_table, lengths, cache_scales, residual, out_weight,
    norm_gain, gate_up, down_weight,
):
    vmem = pl.BlockSpec(memory_space=pltpu.VMEM)
    anywhere = pl.BlockSpec(memory_space=pl.ANY)
    sems = pltpu.SemaphoreType.DMA
    return pl.pallas_call(
        kernel,
        out_shape=jax.ShapeDtypeStruct((8, 512), BF16),
        in_specs=[anywhere] * 11,
        out_specs=vmem,
        scratch_shapes=[
            pltpu.VMEM((4, 1024), BF16),
            pltpu.VMEM((2, 4, 128), BF16),
            pltpu.SMEM((4, 8), jnp.int32),
            pltpu.SMEM((4,), jnp.int32),
            pltpu.SMEM((1, 2), F32),
            pltpu.VMEM((8, 512), BF16),
            pltpu.VMEM((512,), F32),
            pltpu.VMEM((2, 24, 64, 128), BF16),
            pltpu.VMEM((1024, 512), BF16),
            pltpu.VMEM((2, 2, 512, 768), BF16),
            pltpu.VMEM((2, 768, 512), BF16),
            pltpu.VMEM((32, 128), F32),
            pltpu.VMEM((2, 8, 128), F32),
            pltpu.VMEM((16, 32, 128), BF16),
            pltpu.VMEM((8, 16, 256), BF16),
            pltpu.VMEM((8, 16, 256), BF16),
            pltpu.VMEM((8, 512), F32),
            pltpu.VMEM((16, 16, 256), BF16),
            pltpu.VMEM((16, 16, 1536), BF16),
            pltpu.VMEM((16, 16, 1536), BF16),
            pltpu.VMEM((16, 8, 128), F32),
            pltpu.VMEM((16, 8, 128), F32),
            pltpu.VMEM((16, 16, 768), BF16),
            pltpu.VMEM((16, 16, 256), BF16),
            pltpu.VMEM((16, 16, 256), BF16),
            sems((11,)), sems((4,)), sems((2,)), sems((2,)), sems((16,)), sems((2,)), sems((2,)),
            sems((4,)), sems((2,)),
        ],
        compiler_params=pltpu.CompilerParams(
            collective_id=0, has_side_effects=True, vmem_limit_bytes=64 << 20
        ),
        name="decode_layer",
    )(
        queries, fresh_kv, key_value_pages, page_table, lengths, cache_scales.T, residual,
        out_weight, norm_gain, gate_up, down_weight,
    )


def solution(mesh):
    placed = (
        P(("pool", "dp"), "head"),
        P(None, ("pool", "dp"), "head"),
        P(None, ("pool", "dp"), None, "head"),
        P(("pool", "dp"), None),
        P(("pool", "dp")),
        P(None, "head"),
        P(("pool", "head"), "dp"),
        P("head", "dp"),
        P("dp"),
        P(None, "dp", ("pool", "head")),
        P(("pool", "head"), "dp"),
    )
    return jax.shard_map(
        body, mesh=mesh, in_specs=placed, out_specs=P(("pool", "head"), "dp"), check_vma=False
    )
```

time: 82.1 us -> 64.2 us (0.78)
  the two profiles are of different devices: /device:TPU:1 before, /device:TPU:8 now
where the time goes in v2:
time: 64.2 us; the launch traced here: 64 us
  Pallas kernels  62.7 us (98%)
  local copies, waits for them, and re-layouts  1.3 us (2%)
    pallas_call x1, Pallas kernels, body(): pl.pallas_call(kernel, out_shape=jax.ShapeDtypeStruct((8, 512), BF16), in...  62.7 us
    unnamed x1, local copies, waits for them, and re-layouts  1.3 us

profile of v2, /device:TPU:8, one launch (start us, length us, event | category | flops | bytes accessed | tf_op | source)
XLA Modules:
  0.0 64.0 jit_solution(9648209053518062429)
XLA Ops:
  0.0 62.7 %decode_layer.1 = bf16[8,512]{1,0:T(8,128)(2,1)} custom-call(bf16[4,1024]{1,0:T(4,128)(2,1)} %q_hbm.1, bf16[2,4,128]{2,1,0:T(4,128)(2,1)} %fresh_hbm.1, bf16[2,24,64,128]{3,2,1,0:T(8,128)(2,1)} %pages_hbm.1, s32[4,8]{1,0:T(4,128)} %table_hbm.1, s32[4]{0:T(128)} %lengths_hbm.1, f32[1,2]{1,0:T(1,128)} %bitcast.1, bf16[8,512]{1,0:T(8,128)(2,1)} %residual_hbm.1, ...), custom_call_target="tpu_custom_call" | custom-call | tf_op jit(solution)/shard_map/decode_layer/pallas_call | solution.py:285
  62.7 1.3 %copy.13 = bf16[8,512]{1,0:T(8,128)(2,1)} copy(bf16[8,512]{1,0:T(8,128)(2,1)} %decode_layer.1) | data formatting | bytes 16384

commit v3 on v2

--- a/solution.py
+++ b/solution.py
@@ -12,7 +12,7 @@
 MESH = pl.DeviceIdType.MESH
 OFFSETS = (0, 1, -1, 2, -2, 3, -3, 4, -4, 5, -5, 6, -6, 7, -7, 8)
 SLOT = {o % 16: i for i, o in enumerate(OFFSETS)}
-GROUPS = ((0, 1), (1, 3), (3, 7), (7, 11), (11, 16))
+GROUPS = ((0, 1), (1, 3), (3, 8), (8, 12), (12, 16))
 ALONG_Z = (1, -1, 8, 7, -7, 6, -6, 5, -5, 4, -4, 3, -3, 2, -2)
 NEAR = ((0, 1), (0, 3), (1, 0), (3, 0))
 MIDDLE = ((0, 2), (2, 0), (1, 1), (1, 3), (3, 1), (3, 3))
@@ -96,8 +96,10 @@
     q_hbm, fresh_hbm, pages_hbm, table_hbm, lengths_hbm, scales_hbm, residual_hbm, out_w_hbm,
     gain_hbm, gate_up_hbm, down_hbm, out_ref,
     q_ref, fresh_ref, table, lengths, scales, residual_ref, gain_ref, kv, out_w, gate_up, down, q_rows, fresh_rows, att, b_send, b_recv, stream, normed,
-    d_send, d_recv, sq_send, sq_recv, hidden, g_send, g_recv,
-    load_sem, pair_sem, a_sem, b_sem, c_sem, d_sem, sq_sem, h_sem, g_sem,
+    d_send, d_recv, sq_send, sq_recv, scale_send, scale_recv, hidden,
+    g_send, g_recv,
+    load_sem, pair_sem, a_sem, b_sem, c_sem, d_sem, sq_sem, scale_sem,
+    h_sem, g_sem,
 ):
     z, core, y, x = place()
     dp = y * 4 + x
@@ -178,88 +180,109 @@
         slot = SLOT[-k % 16]
         send(normed.at[0], normed.at[slot], c_sem.at[0], c_sem.at[slot], ring(k))
 
-    inverse = 1.0 / (gain * gain)
+    squares = stream[...] * stream[...]
+    sq_send[...] = squares[:, :128] + squares[:, 128:256] + squares[:, 256:384] + squares[:, 384:]
+    for step in others:
+        send(sq_send, sq_recv.at[dp], sq_sem.at[0], sq_sem.at[1], plane(*step))
+    sq_recv[dp] = sq_send[...]
+
+    unit = ((x - y + 4) % 4) * 4 + y
+    unit_chip, unit_core = unit // 2, unit % 2
+
+    def unit_ring(phase):
+        slot = 8 * phase + unit_chip
+        return ((slot + 1) // 2) * (2 * (slot % 2) - 1)
+
+    def scales_out():
+        wait(sq_recv.at[0:15], sq_sem.at[1])
+        mean = jnp.sum(jnp.sum(sq_recv[...], axis=0), axis=1, keepdims=True) / D
+        scale_send[...] = jnp.broadcast_to(lax.rsqrt(mean + 1e-6), (8, 128))
+        send(scale_send, scale_recv.at[1], scale_sem.at[0], scale_sem.at[2], ring(-unit_ring(1)))
+
+        @pl.when(unit_chip != 0)
+        def _():
+            send(scale_send, scale_recv.at[0], scale_sem.at[0], scale_sem.at[1], ring(-unit_ring(0)))
+
+        @pl.when(unit_chip == 0)
+        def _():
+            scale_recv[0] = scale_send[...]
 
     def feed(group):
         lo, hi = GROUPS[group]
         n = hi - lo
         for slot in range(max(lo, 1), hi):
             wait(normed.at[0], c_sem.at[slot])
-        tokens = from_tile(normed[lo:hi]).reshape(8 * n, 512)
-        squares = tokens * tokens * inverse
-        squares = squares[:, :128] + squares[:, 128:256] + squares[:, 256:384] + squares[:, 384:]
-        sq_send[lo:hi] = squares.reshape(n, 8, 128)
-        lhs = tokens.astype(BF16)
-
-        def both(i):
-            parts = [jnp.dot(lhs, gate_up[c, i], preferred_element_type=F32) for c in range(2)]
-            return jnp.concatenate(parts, axis=1).reshape(n, 8, 1536)
-
-        d_send[lo:hi] = jnp.concatenate([both(0), both(1)], axis=1).astype(BF16)
+        lhs = from_tile(normed[lo:hi]).reshape(8 * n, 512).astype(BF16)
+        for c in range(2):
+            gate = jnp.dot(lhs, gate_up[c, 0], preferred_element_type=F32).reshape(n, 8, 768)
+            up = jnp.dot(lhs, gate_up[c, 1], preferred_element_type=F32).reshape(n, 8, 768)
+            d_send[c, lo:hi] = jnp.concatenate([gate, up], axis=1).astype(BF16)
         for slot in range(lo, hi):
-            u = OFFSETS[slot] % 16
-            oy, ox = u % 4, (u % 4 + u // 4) % 4
-            same = dp == oy * 4 + ox
-
-            @pl.when(jnp.logical_not(same))
+            phase = slot // 8
+            for c in range(2):
+                u = 2 * (slot % 8) + c
+                oy, ox = u % 4, (u % 4 + u // 4) % 4
+                same = dp == oy * 4 + ox
+
+                @pl.when(jnp.logical_not(same))
+                def _():
+                    send(
+                        d_send.at[c, slot], d_recv.at[phase, dp], d_sem.at[0], d_sem.at[1 + phase],
+                        device(z, core, oy, ox),
+                    )
+
+                @pl.when(same)
+                def _():
+                    d_recv[phase, dp] = d_send[c, slot]
+
+    def share_hidden(phase):
+        if phase == 0:
+
+            @pl.when(unit_chip != 0)
             def _():
-                to = device(z, core, oy, ox)
-                send(d_send.at[slot], d_recv.at[dp], d_sem.at[0], d_sem.at[1], to)
-                send(sq_send.at[slot], sq_recv.at[dp], sq_sem.at[0], sq_sem.at[1], to)
-
-            @pl.when(same)
-            def _():
-                d_recv[dp] = d_send[slot]
-                sq_recv[dp] = sq_send[slot]
+                wait(scale_send, scale_sem.at[1])
+        else:
+            wait(scale_send, scale_sem.at[2])
+        scale = scale_recv[phase][:, :1]
+        wait(d_recv.at[0, 0:15], d_sem.at[1 + phase])
+        total = d_recv[phase, 0].astype(F32)
+        for i in range(1, 16):
+            total = total + d_recv[phase, i].astype(F32)
+        gate, up = total[:8] * scale, total[8:] * scale
+        own = gate / (1.0 + jnp.exp(-gate)) * up
+        hidden[phase, unit_core, unit_chip] = jnp.concatenate([own[:, :384], own[:, 384:]], axis=0).astype(BF16)
+        mine = hidden.at[phase, unit_core, unit_chip]
+        for step in others:
+            send(mine, mine, h_sem.at[0], h_sem.at[1 + phase], plane(*step))
+
+    def lower(phase):
+        wait(d_recv.at[0, 0:15, :, 0:384], h_sem.at[1 + phase])
+        lowered = jnp.zeros((64, 512), F32)
+        for c in range(2):
+            tokens = hidden[phase, c].astype(F32)
+            lhs = jnp.concatenate([tokens[:, :8], tokens[:, 8:]], axis=2).reshape(64, 768).astype(BF16)
+            lowered = lowered + jnp.dot(lhs, down[c], preferred_element_type=F32)
+        g_send[8 * phase : 8 * phase + 8] = to_tile(lowered.reshape(8, 8, 512))
+        for slot in range(8 * phase + 7, 8 * phase - 1, -1):
+            if slot == 0:
+                g_recv[0] = g_send[0]
+            else:
+                send(g_send.at[slot], g_recv.at[slot], g_sem.at[0], g_sem.at[1], ring(OFFSETS[slot]))
 
     loads[9].wait()
     wait(gate_up.at[0], pair_sem.at[1])
-    for group in range(5):
-        feed(group)
-
-    own = ((x - y + 4) % 4) * 4 + y
-    wait(sq_recv.at[0:15], sq_sem.at[1])
-    mean = jnp.sum(jnp.sum(sq_recv[...], axis=0), axis=1, keepdims=True) / D
-    scale = lax.rsqrt(mean + 1e-6)
-    wait(d_recv.at[0:15], d_sem.at[1])
-    total = d_recv[0].astype(F32)
-    for i in range(1, 16):
-        total = total + d_recv[i].astype(F32)
-    gate, up = total[:8] * scale, total[8:] * scale
-    own_hidden = gate / (1.0 + jnp.exp(-gate)) * up
-    hidden[own] = jnp.concatenate([own_hidden[:, :768], own_hidden[:, 768:]], axis=0).astype(BF16)
-    mine = hidden.at[own]
-    for steps, sem in ((FAR[::-1], 3), (MIDDLE, 2), (NEAR, 1)):
-        for dy, dx in steps:
-            send(mine, mine, h_sem.at[0], h_sem.at[sem], plane(-dy, -dx))
+    feed(0)
+    feed(1)
+    scales_out()
+    feed(2)
+    feed(3)
+    feed(4)
+    share_hidden(0)
+    share_hidden(1)
     loads[10].wait()
     wait(down.at[0], pair_sem.at[3])
-
-    def lower(start, steps):
-        n = len(steps)
-        chips = [((x + dx - y - dy + 8) % 4) * 4 + (y + dy) % 4 for dy, dx in steps]
-        tokens = jnp.concatenate([hidden[u][None] for u in chips], axis=0).astype(F32)
-        lowered = jnp.zeros((8 * n, 512), F32)
-        for c in range(2):
-            lhs = tokens[:, 8 * c : 8 * c + 8].reshape(8 * n, 768).astype(BF16)
-            lowered = lowered + jnp.dot(lhs, down[c], preferred_element_type=F32)
-        g_send[pl.ds(start, n)] = to_tile(lowered.reshape(n, 8, 512))
-        for i, u in enumerate(chips):
-
-            @pl.when(u != 0)
-            def _():
-                send(g_send.at[start + i], g_recv.at[u], g_sem.at[0], g_sem.at[1], ring(u))
-
-            @pl.when(u == 0)
-            def _():
-                g_recv[0] = g_send[start + i]
-
-    wait(hidden.at[0:4], h_sem.at[1])
-    lower(0, ((0, 0),) + NEAR)
-    wait(hidden.at[0:6], h_sem.at[2])
-    lower(5, MIDDLE)
-    wait(hidden.at[0:5], h_sem.at[3])
-    lower(11, FAR)
+    lower(0)
+    lower(1)
     wait(g_recv.at[1:16], g_sem.at[1])
     lowered = from_tile(jnp.sum(g_recv[...].astype(F32), axis=0))
     out_ref[...] = (stream[...] + lowered).astype(BF16)
@@ -269,9 +292,15 @@
     wait(att.at[0:15], a_sem.at[0])
     wait(b_recv.at[0:7], b_sem.at[0])
     wait(normed.at[0:15], c_sem.at[0])
-    wait(d_recv.at[0:15], d_sem.at[0])
+    wait(d_recv.at[:, 0:15], d_sem.at[0])
     wait(sq_recv.at[0:15], sq_sem.at[0])
-    wait(hidden.at[0:15], h_sem.at[0])
+    wait(scale_send, scale_sem.at[0])
+
+    @pl.when(unit_chip != 0)
+    def _():
+        wait(scale_send, scale_sem.at[0])
+
+    wait(d_recv.at[0, 0:15], h_sem.at[0])
     wait(g_recv.at[0:15], g_sem.at[0])
 
 
@@ -306,15 +335,17 @@
             pltpu.VMEM((8, 16, 256), BF16),
             pltpu.VMEM((8, 512), F32),
             pltpu.VMEM((16, 16, 256), BF16),
-            pltpu.VMEM((16, 16, 1536), BF16),
-            pltpu.VMEM((16, 16, 1536), BF16),
+            pltpu.VMEM((2, 16, 16, 768), BF16),
+            pltpu.VMEM((2, 16, 16, 768), BF16),
+            pltpu.VMEM((8, 128), F32),
             pltpu.VMEM((16, 8, 128), F32),
-            pltpu.VMEM((16, 8, 128), F32),
-            pltpu.VMEM((16, 16, 768), BF16),
+            pltpu.VMEM((8, 128), F32),
+            pltpu.VMEM((2, 8, 128), F32),
+            pltpu.VMEM((2, 2, 8, 16, 384), BF16),
             pltpu.VMEM((16, 16, 256), BF16),
             pltpu.VMEM((16, 16, 256), BF16),
-            sems((11,)), sems((4,)), sems((2,)), sems((2,)), sems((16,)), sems((2,)), sems((2,)),
-            sems((4,)), sems((2,)),
+            sems((11,)), sems((4,)), sems((2,)), sems((2,)), sems((16,)), sems((3,)), sems((2,)),
+            sems((3,)), sems((3,)), sems((2,)),
         ],
         compiler_params=pltpu.CompilerParams(
             collective_id=0, has_side_effects=True, vmem_limit_bytes=64 << 20

time: 64.2 us -> 61.7 us (0.961)
  the two profiles are of different devices: /device:TPU:8 before, /device:TPU:32 now
where the time goes in v3:
time: 61.7 us; the launch traced here: 61.5 us
  Pallas kernels  60.2 us (98%)
  local copies, waits for them, and re-layouts  1.3 us (2%)
    pallas_call x1, Pallas kernels, body(): pl.pallas_call(kernel, out_shape=jax.ShapeDtypeStruct((8, 512), BF16), in...  60.2 us
    unnamed x1, local copies, waits for them, and re-layouts  1.3 us

profile of v3, /device:TPU:32, one launch (start us, length us, event | category | flops | bytes accessed | tf_op | source)
XLA Modules:
  0.0 61.5 jit_solution(14608679087148139720)
XLA Ops:
  0.0 60.2 %decode_layer.1 = bf16[8,512]{1,0:T(8,128)(2,1)} custom-call(bf16[4,1024]{1,0:T(4,128)(2,1)} %q_hbm.1, bf16[2,4,128]{2,1,0:T(4,128)(2,1)} %fresh_hbm.1, bf16[2,24,64,128]{3,2,1,0:T(8,128)(2,1)} %pages_hbm.1, s32[4,8]{1,0:T(4,128)} %table_hbm.1, s32[4]{0:T(128)} %lengths_hbm.1, f32[1,2]{1,0:T(1,128)} %bitcast.1, bf16[8,512]{1,0:T(8,128)(2,1)} %residual_hbm.1, ...), custom_call_target="tpu_custom_call" | custom-call | tf_op jit(solution)/shard_map/decode_layer/pallas_call | solution.py:314
  60.2 1.3 %copy.13 = bf16[8,512]{1,0:T(8,128)(2,1)} copy(bf16[8,512]{1,0:T(8,128)(2,1)} %decode_layer.1) | data formatting | bytes 16384

commit v4 on v3

--- a/solution.py
+++ b/solution.py
@@ -12,7 +12,7 @@
 MESH = pl.DeviceIdType.MESH
 OFFSETS = (0, 1, -1, 2, -2, 3, -3, 4, -4, 5, -5, 6, -6, 7, -7, 8)
 SLOT = {o % 16: i for i, o in enumerate(OFFSETS)}
-GROUPS = ((0, 1), (1, 3), (3, 8), (8, 12), (12, 16))
+GROUPS = ((0, 3), (3, 8), (8, 16))
 ALONG_Z = (1, -1, 8, 7, -7, 6, -6, 5, -5, 4, -4, 3, -3, 2, -2)
 NEAR = ((0, 1), (0, 3), (1, 0), (3, 0))
 MIDDLE = ((0, 2), (2, 0), (1, 1), (1, 3), (3, 1), (3, 3))
@@ -130,7 +130,7 @@
     def greet(to):
         pl.semaphore_signal(barrier, inc=1, device_id=to, device_id_type=MESH)
 
-    for k in range(1, 16):
+    for k in sorted(ALONG_Z, key=abs, reverse=True):
         greet(ring(k))
     for step in others:
         greet(plane(*step))
@@ -143,7 +143,6 @@
     for step in others:
         send(att.at[dp], att.at[dp], a_sem.at[0], a_sem.at[1], plane(*step))
     send(gate_up_hbm, gate_up.at[core], pair_sem.at[0], pair_sem.at[1], sibling)
-    send(down_hbm, down.at[core], pair_sem.at[2], pair_sem.at[3], sibling)
     for load in loads[6:9]:
         load.wait()
     wait(att.at[0:15], a_sem.at[1])
@@ -170,6 +169,7 @@
         to = jnp.where(head < 4, up_to, down_to)
         send(b_send.at[to], b_recv.at[head], b_sem.at[0], b_sem.at[1], device((z // 8) * 8 + to, core, y, x))
     b_recv[head] = b_send[head]
+    send(down_hbm, down.at[core], pair_sem.at[2], pair_sem.at[3], sibling)
     wait(b_recv.at[0:7], b_sem.at[1])
     summed = from_tile(jnp.sum(b_recv[...].astype(F32), axis=0))
     stream[...] = residual_ref[...].astype(F32) + summed
@@ -275,8 +275,6 @@
     feed(1)
     scales_out()
     feed(2)
-    feed(3)
-    feed(4)
     share_hidden(0)
     share_hidden(1)
     loads[10].wait()

time: 61.7 us -> 61 us (0.989)
  Pallas kernels: 60.2 us -> 59.5 us
    pallas_call x1, Pallas kernels: 60.2 us -> 59.5 us  [body(): pl.pallas_call(kernel, out_shape=jax.ShapeDtypeStruct((8, 512), BF16), in...]
where the time goes in v4:
time: 61 us; the launch traced here: 60.8 us
  Pallas kernels  59.5 us (98%)
  local copies, waits for them, and re-layouts  1.3 us (2%)
    pallas_call x1, Pallas kernels, body(): pl.pallas_call(kernel, out_shape=jax.ShapeDtypeStruct((8, 512), BF16), in...  59.5 us
    unnamed x1, local copies, waits for them, and re-layouts  1.3 us

profile of v4, /device:TPU:32, one launch (start us, length us, event | category | flops | bytes accessed | tf_op | source)
XLA Modules:
  0.0 60.8 jit_solution(7376569319026097475)
XLA Ops:
  0.0 59.5 %decode_layer.1 = bf16[8,512]{1,0:T(8,128)(2,1)} custom-call(bf16[4,1024]{1,0:T(4,128)(2,1)} %q_hbm.1, bf16[2,4,128]{2,1,0:T(4,128)(2,1)} %fresh_hbm.1, bf16[2,24,64,128]{3,2,1,0:T(8,128)(2,1)} %pages_hbm.1, s32[4,8]{1,0:T(4,128)} %table_hbm.1, s32[4]{0:T(128)} %lengths_hbm.1, f32[1,2]{1,0:T(1,128)} %bitcast.1, bf16[8,512]{1,0:T(8,128)(2,1)} %residual_hbm.1, ...), custom_call_target="tpu_custom_call" | custom-call | tf_op jit(solution)/shard_map/decode_layer/pallas_call | solution.py:312
  59.5 1.3 %copy.13 = bf16[8,512]{1,0:T(8,128)(2,1)} copy(bf16[8,512]{1,0:T(8,128)(2,1)} %decode_layer.1) | data formatting | bytes 16384

commit v5 on v4

--- a/solution.py
+++ b/solution.py
@@ -217,10 +217,8 @@
             gate = jnp.dot(lhs, gate_up[c, 0], preferred_element_type=F32).reshape(n, 8, 768)
             up = jnp.dot(lhs, gate_up[c, 1], preferred_element_type=F32).reshape(n, 8, 768)
             d_send[c, lo:hi] = jnp.concatenate([gate, up], axis=1).astype(BF16)
-        for slot in range(lo, hi):
-            phase = slot // 8
-            for c in range(2):
-                u = 2 * (slot % 8) + c
+            for slot in range(lo, hi):
+                phase, u = slot // 8, 2 * (slot % 8) + c
                 oy, ox = u % 4, (u % 4 + u // 4) % 4
                 same = dp == oy * 4 + ox
 

time: 61 us -> 61.3 us (level)
  no operation moved by 1% of the time
where the time goes in v5:
time: 61.3 us; the launch traced here: 61.1 us
  Pallas kernels  59.8 us (98%)
  local copies, waits for them, and re-layouts  1.3 us (2%)
    pallas_call x1, Pallas kernels, body(): pl.pallas_call(kernel, out_shape=jax.ShapeDtypeStruct((8, 512), BF16), in...  59.8 us
    unnamed x1, local copies, waits for them, and re-layouts  1.3 us

profile of v5, /device:TPU:32, one launch (start us, length us, event | category | flops | bytes accessed | tf_op | source)
XLA Modules:
  0.0 61.1 jit_solution(14312693981924557661)
XLA Ops:
  0.0 59.8 %decode_layer.1 = bf16[8,512]{1,0:T(8,128)(2,1)} custom-call(bf16[4,1024]{1,0:T(4,128)(2,1)} %q_hbm.1, bf16[2,4,128]{2,1,0:T(4,128)(2,1)} %fresh_hbm.1, bf16[2,24,64,128]{3,2,1,0:T(8,128)(2,1)} %pages_hbm.1, s32[4,8]{1,0:T(4,128)} %table_hbm.1, s32[4]{0:T(128)} %lengths_hbm.1, f32[1,2]{1,0:T(1,128)} %bitcast.1, bf16[8,512]{1,0:T(8,128)(2,1)} %residual_hbm.1, ...), custom_call_target="tpu_custom_call" | custom-call | tf_op jit(solution)/shard_map/decode_layer/pallas_call | solution.py:310
  59.8 1.3 %copy.13 = bf16[8,512]{1,0:T(8,128)(2,1)} copy(bf16[8,512]{1,0:T(8,128)(2,1)} %decode_layer.1) | data formatting | bytes 16384
